TPU v7x, 256 devices: a whole 4x4x8 slice. The times are simulated.
256 devices in a mesh: gx: 8 (over x, core), gy: 4 (over y), gz: 8 (over z).
Axes of the slice: x: 4, y: 4, z: 8, core: 2. Of those that a mesh axis runs over, the one named last changes fastest.
Arguments:
- field: bfloat16 [64, 64, 64, 128], P('gx', 'gy', 'gz'), may hold values from -6 to 6
- coarse_weight: bfloat16 [27, 128, 256], replicated, may hold values from -0.109375 to 0.109375
- fine_weight: bfloat16 [27, 256, 128], replicated, may hold values from -0.078125 to 0.078125
- cotangent: bfloat16 [64, 64, 64, 128], P('gx', 'gy', 'gz'), may hold values from -6 to 6
Outputs:
- output: bfloat16 [64, 64, 64, 128], P('gx', 'gy', 'gz')
- field_grad: bfloat16 [64, 64, 64, 128], P('gx', 'gy', 'gz')
- fine_grad: float32 [27, 256, 128], P(None, None, 'gz')
- coarse_grad: float32 [27, 128, 256], P(None, None, 'gz')
All inputs are finite; a program needn't handle non-finite values.
Results may differ from a plain program's by a relative error of at most 0.0051.
Values may be sent and summed in bfloat16 or wider, within the bound.
A program may use at most 128 MiB of HBM per device.

v0:
```python
import math

import jax
import jax.numpy as jnp
from jax import lax
from jax.experimental import pallas as pl
from jax.experimental.pallas import tpu as pltpu
from jax.sharding import PartitionSpec as P

MESH = pl.DeviceIdType.MESH
F32 = jnp.float32
BF16 = jnp.bfloat16

EIGHT = [(i, j) for i in (-1, 0, 1) for j in (-1, 0, 1) if (i, j) != (0, 0)]
PAIRS = ((0,), (1, 2), (0, 1), (2,))


def from_side(step, length):
    return pl.ds(1, length) if step == 0 else pl.ds(length if step > 0 else 1, 1)


def to_side(step, length):
    return pl.ds(1, length) if step == 0 else pl.ds(0 if step > 0 else length + 1, 1)


def make_kernel(sizes):
    nx, ny, nz = sizes
    chips = nx // 2
    cells = 1024 * nx * ny * nz

    def kernel(
        field_hbm, w1_hbm, w2_hbm, cot_hbm,
        out_ref, grad_ref, fine_ref, coarse_ref,
        field_v, cot_v, w1, w2, wc,
        cp, zs, zr, tmp, pool_b, pool_s, pool_r, hid_b, hid_s, hid_r, dp_b, dp_s, dp_r,
        im, hb, hi, di, ob, fg,
        g, a1, a2, a3s, a3, r1, b1, b2, b3s, b3, r2, zb, ag,
        in_sem, halo_send, halo_recv, pair_send, pair_recv, rs_send, rs_recv, z_send, z_recv, ag_send, ag_recv,
    ):
        gx, gy, gz = lax.axis_index("gx"), lax.axis_index("gy"), lax.axis_index("gz")
        core = lax.rem(gx, 2)
        chip = gx // 2

        def at(dx, dy, dz):
            return (
                lax.rem(gx + (dx + nx), nx),
                lax.rem(gy + (dy + ny), ny),
                lax.rem(gz + (dz + nz), nz),
            )

        def remote(src, dst, send, recv, device):
            copy = pltpu.make_async_remote_copy(
                src_ref=src, dst_ref=dst, send_sem=send, recv_sem=recv, device_id=device, device_id_type=MESH
            )
            copy.start()
            return copy

        sent = []

        loads = [
            pltpu.make_async_copy(src, dst, in_sem.at[i])
            for i, (src, dst) in enumerate(
                ((field_hbm, field_v), (cot_hbm, cot_v), (w2_hbm, w2), (w1_hbm, w1))
            )
        ]
        for load in loads:
            load.start()

        partners = {(i, j, 0) for i, j in EIGHT} | {(i, 0, j) for i, j in EIGHT} | {(0, 0, 1), (0, 0, nz - 1)}
        partners = {(i % nx, j % ny, k % nz) for i, j, k in partners}
        partners |= {(0, 0, k) for k in range(1, nz)}
        partners |= {(2 * i, j, 0) for i in range(chips) for j in range(ny) if (i, j) != (0, 0)}
        barrier = pltpu.get_barrier_semaphore()
        for step in sorted(partners):
            pl.semaphore_signal(barrier, inc=1, device_id=at(*step), device_id_type=MESH)

        loads[0].wait()
        for x in range(4):
            pair = field_v[2 * x].astype(F32) + field_v[2 * x + 1].astype(F32)
            pair = pair.reshape(8, 2, 8, 128)
            tmp[x] = (pair[:, 0] + pair[:, 1]).reshape(64, 128)
        for z in range(4):
            total = tmp[:, pl.ds(2 * z, 8, stride=8), :] + tmp[:, pl.ds(2 * z + 1, 8, stride=8), :]
            pool_b[0, 1:5, 1 + z, 8:16, :] = (total * 0.125).astype(BF16).astype(F32)
        loads[1].wait()
        for x in range(8):
            cp[1 + x, 8:136, :] = cot_v[x].astype(F32)

        pl.semaphore_wait(barrier, len(partners))

        def start_xz(buf, e):
            copies = []
            for i, (dx, dz) in enumerate(EIGHT):
                copies.append(
                    remote(
                        buf.at[:, from_side(dx, 4), from_side(dz, 4), pl.ds(8, 8), :],
                        buf.at[:, to_side(dx, 4), to_side(dz, 4), pl.ds(8, 8), :],
                        halo_send.at[e, i], halo_recv.at[e, i], at(dx, 0, dz),
                    )
                )
            sent.extend(copies)
            return copies

        def start_y(buf, s, r, e, copies):
            for copy in copies:
                copy.wait_recv()

            @pl.when(gx == 0)
            def _():
                buf[:, 0, :, 8:16, :] = jnp.zeros_like(buf[:, 0, :, 8:16, :])

            @pl.when(gx == nx - 1)
            def _():
                buf[:, 5, :, 8:16, :] = jnp.zeros_like(buf[:, 5, :, 8:16, :])

            @pl.when(gz == 0)
            def _():
                buf[:, :, 0, 8:16, :] = jnp.zeros_like(buf[:, :, 0, 8:16, :])

            @pl.when(gz == nz - 1)
            def _():
                buf[:, :, 5, 8:16, :] = jnp.zeros_like(buf[:, :, 5, 8:16, :])

            flat = buf.reshape(buf.shape[0], 864, 128)
            for h in range(buf.shape[0]):
                s[0, h, 0:36, :] = flat[h, pl.ds(8, 36, stride=24), :]
                s[1, h, 0:36, :] = flat[h, pl.ds(15, 36, stride=24), :]
            below = remote(s.at[0], r.at[1], halo_send.at[e, 8], halo_recv.at[e, 8], at(0, -1, 0))
            above = remote(s.at[1], r.at[0], halo_send.at[e, 9], halo_recv.at[e, 9], at(0, 1, 0))
            sent.extend((below, above))
            return (above, below)

        def finish_y(buf, r, copies):
            for copy in copies:
                copy.wait_recv()

            @pl.when(gy == 0)
            def _():
                r[0] = jnp.zeros_like(r[0])

            @pl.when(gy == ny - 1)
            def _():
                r[1] = jnp.zeros_like(r[1])

            flat = buf.reshape(buf.shape[0], 864, 128)
            for h in range(buf.shape[0]):
                flat[h, pl.ds(7, 36, stride=24), :] = r[0, h, 0:36, :]
                flat[h, pl.ds(16, 36, stride=24), :] = r[1, h, 0:36, :]

        def tap(buf, h, a, b, c):
            return buf[h, a : a + 4, c : c + 4, 7 + b : 15 + b, :].reshape(128, 128).astype(BF16)

        pool_xz = start_xz(pool_b, 0)
        cot_xy = []
        for i, (dx, dy) in enumerate(EIGHT):
            sy = pl.ds(8, 128) if dy == 0 else pl.ds(128 if dy > 0 else 8, 8)
            ty = pl.ds(8, 128) if dy == 0 else pl.ds(0 if dy > 0 else 136, 8)
            cot_xy.append(
                remote(
                    cp.at[from_side(dx, 8), sy, :], cp.at[to_side(dx, 8), ty, :],
                    halo_send.at[3, i], halo_recv.at[3, i], at(dx, dy, 0),
                )
            )
        sent.extend(cot_xy)

        pool_y = start_y(pool_b, pool_s, pool_r, 0, pool_xz)

        for copy in cot_xy:
            copy.wait_recv()

        @pl.when(gx == 0)
        def _():
            cp[0] = jnp.zeros_like(cp[0])

        @pl.when(gx == nx - 1)
        def _():
            cp[9] = jnp.zeros_like(cp[9])

        @pl.when(gy == 0)
        def _():
            cp[:, 0:8, :] = jnp.zeros_like(cp[:, 0:8, :])

        @pl.when(gy == ny - 1)
        def _():
            cp[:, 136:144, :] = jnp.zeros_like(cp[:, 136:144, :])

        cp[:, 144:192, :] = jnp.zeros_like(cp[:, 144:192, :])
        zs[0] = cp[:, pl.ds(0, 24, stride=8), :]
        zs[1] = cp[:, pl.ds(7, 24, stride=8), :]
        z_below = remote(zs.at[0], zr.at[1], halo_send.at[3, 8], halo_recv.at[3, 8], at(0, 0, -1))
        z_above = remote(zs.at[1], zr.at[0], halo_send.at[3, 9], halo_recv.at[3, 9], at(0, 0, 1))
        sent.extend((z_below, z_above))

        loads[2].wait()

        def combine(i, carry):
            rows = pl.ds(pl.multiple_of(i * 16, 16), 16)
            low = pl.ds(pl.multiple_of(i * 16, 16), 16)
            high = pl.ds(pl.multiple_of(256 + i * 16, 16), 16)

            def spread(parts):
                return (parts[0], parts[1] + parts[2], parts[0] + parts[1], parts[2])

            by_ab = [[spread([w2[9 * a + 3 * b + c, rows, :].astype(F32) for c in range(3)]) for b in range(3)] for a in range(3)]
            by_a = [[spread([by_ab[a][b][c] for b in range(3)]) for c in range(4)] for a in range(3)]
            for b in range(4):
                for c in range(4):
                    for a, value in enumerate(spread([by_a[a][c][b] for a in range(3)])):
                        parity = (a // 2) * 4 + (b // 2) * 2 + c // 2
                        wc[parity, (a % 2) * 2 + b % 2, high if c % 2 else low, :] = value.astype(BF16)
            return carry

        lax.fori_loop(0, 16, combine, 0)

        finish_y(pool_b, pool_r, pool_y)
        for k in range(27):
            im[0, 0:128, k * 128 : (k + 1) * 128] = tap(pool_b, 0, k // 9, k // 3 % 3, k % 3)
        loads[3].wait()
        pre = jnp.dot(im[0, 0:128, :], w1[...].reshape(3456, 256), preferred_element_type=F32)
        sig = 1.0 / (1.0 + jnp.exp(-pre))
        hidden = (pre * sig).astype(BF16)
        slope = sig * (1.0 + pre * (1.0 - sig))
        hb[1, 0:128, :] = hidden
        wide = hidden.astype(F32).reshape(4, 4, 8, 256)
        hid_b[0, 1:5, 1:5, 8:16, :] = wide[..., 0:128]
        hid_b[1, 1:5, 1:5, 8:16, :] = wide[..., 128:256]
        hid_xz = start_xz(hid_b, 1)

        z_below.wait_recv()
        z_above.wait_recv()

        @pl.when(gz == 0)
        def _():
            zr[0] = jnp.zeros_like(zr[0])

        @pl.when(gz == nz - 1)
        def _():
            zr[1] = jnp.zeros_like(zr[1])

        def windows(x, carry):
            rows = pl.ds(pl.multiple_of(x * 32, 32), 32)
            for a in range(3):
                planes = pl.ds(2 * x + 2 - a, 2)
                sums = []
                for z in range(10):
                    columns = []
                    for y in range(4):
                        if z == 0:
                            value = zr[0, planes, pl.ds(y, 8, stride=2), :]
                        elif z == 9:
                            value = zr[1, planes, pl.ds(y, 8, stride=2), :]
                        else:
                            value = cp[planes, pl.ds(y * 8 + z - 1, 8, stride=16), :]
                        columns.append(value[0] + value[1])
                    sums.append([columns[2 - b] + columns[3 - b] for b in range(3)])
                for b in range(3):
                    for c in range(3):
                        k = 9 * a + 3 * b + c
                        value = jnp.concatenate(
                            [sums[2 * z + 2 - c][b] + sums[2 * z + 3 - c][b] for z in range(4)], axis=0
                        )
                        im[1, rows, k * 128 : (k + 1) * 128] = value.astype(BF16)
            return carry

        lax.fori_loop(0, 4, windows, 0)

        other = (gx + 1 - 2 * core, gy, gz)
        pair_im = remote(
            im.at[core, pl.ds(0, 128), :], im.at[core, pl.ds(128, 128), :], pair_send.at[0], pair_recv.at[0], other
        )

        d_hidden = jnp.zeros((128, 256), F32)
        for k in range(27):
            d_hidden = d_hidden + lax.dot_general(
                im[1, 0:128, k * 128 : (k + 1) * 128], w2[k], (((1,), (1,)), ((), ())), preferred_element_type=F32
            )
        d_pre = (d_hidden * slope).astype(BF16)
        hb[0, 0:128, :] = d_pre
        pair_hb = remote(
            hb.at[core, pl.ds(0, 128), :], hb.at[core, pl.ds(128, 128), :], pair_send.at[1], pair_recv.at[1], other
        )
        wide = d_pre.astype(F32).reshape(4, 4, 8, 256)
        dp_b[0, 1:5, 1:5, 8:16, :] = wide[..., 0:128]
        dp_b[1, 1:5, 1:5, 8:16, :] = wide[..., 128:256]
        dp_xz = start_xz(dp_b, 2)
        hid_y = start_y(hid_b, hid_s, hid_r, 1, hid_xz)

        pair_im.wait_recv()
        pair_hb.wait_recv()
        g[:, :, 27] = jnp.zeros((2, 8, 16, 128), BF16)

        @pl.when(core == 0)
        def _():
            right = hb[1]
            for k in range(27):
                value = lax.dot_general(
                    im[1, :, k * 128 : (k + 1) * 128], right, (((0,), (0,)), ((), ())), preferred_element_type=F32
                ).astype(BF16)
                value = value.reshape(8, 16, 256)
                g[0, :, k] = value[..., 0:128]
                g[1, :, k] = value[..., 128:256]

        @pl.when(core == 1)
        def _():
            left = hb[0].astype(F32).T.astype(BF16)
            for k in range(27):
                value = jnp.dot(left, im[0, :, k * 128 : (k + 1) * 128], preferred_element_type=F32).astype(BF16)
                value = value.reshape(8, 2, 16, 128)
                g[0, :, k] = value[:, 0]
                g[1, :, k] = value[:, 1]

        def ring(axis, step):
            return at(2 * step, 0, 0) if axis == 0 else at(0, step, 0)

        def place(axis, step):
            return lax.rem(chip + step + 4, 4) if axis == 0 else lax.rem(gy + step + 4, 4)

        def rs_first(src, first, second, units, stage):
            waiting = {}
            for h in range(2):
                axis = (h + stage) % 2
                for i, d in enumerate((1, -1)):
                    waiting[h, i] = (
                        remote(
                            src.at[h, pl.ds(4 * i, 4), pl.ds(units * place(axis, 2), units)], first.at[h, i],
                            rs_send.at[stage, h, i, 0], rs_recv.at[stage, h, i, 0], ring(axis, d),
                        ),
                        remote(
                            src.at[h, pl.ds(4 - 4 * i, 4), pl.ds(units * place(axis, d), units)], second.at[h, i],
                            rs_send.at[stage, h, i, 1], rs_recv.at[stage, h, i, 1], ring(axis, d),
                        ),
                    )
                    sent.extend(waiting[h, i])
            return waiting

        def rs_relay(src, first, out, third, units, stage, waiting):
            relays = {}
            for h in range(2):
                axis = (h + stage) % 2
                for i, d in enumerate((1, -1)):
                    waiting[h, i][0].wait_recv()
                    mine = src[h, 4 * i : 4 * i + 4, pl.ds(units * place(axis, d), units)]
                    out[h, i] = (mine.astype(F32) + first[h, i].astype(F32)).astype(BF16)
                    relays[h, i] = remote(
                        out.at[h, i], third.at[h, i],
                        rs_send.at[stage, h, i, 2], rs_recv.at[stage, h, i, 2], ring(axis, d),
                    )
                    sent.append(relays[h, i])
            return relays

        def rs_last(src, second, third, units, stage, waiting, relays, h, i):
            axis = (h + stage) % 2
            waiting[h, 1 - i][1].wait_recv()
            relays[h, i].wait_recv()
            mine = src[h, 4 * i : 4 * i + 4, pl.ds(units * place(axis, 0), units)]
            total = mine.astype(F32) + second[h, 1 - i].astype(F32) + third[h, i].astype(F32)
            return total.astype(BF16)

        first = rs_first(g, a1, a2, 7, 0)

        dp_y = start_y(dp_b, dp_s, dp_r, 2, dp_xz)
        finish_y(hid_b, hid_r, hid_y)
        for k in range(27):
            for h in range(2):
                hi[:, k * 256 + h * 128 : k * 256 + (h + 1) * 128] = tap(hid_b, h, k // 9, k // 3 % 3, k % 3)

        relays = rs_relay(g, a1, a3s, a3, 7, 0, first)

        for parity in range(8):
            pa, pb, pc = parity // 4, parity // 2 % 2, parity % 2
            total = jnp.zeros((128, 128), F32)
            for side in range(4):
                k = 9 * (pa + side // 2) + 3 * (pb + side % 2) + pc
                total = total + jnp.dot(hi[:, k * 256 : k * 256 + 512], wc[parity, side], preferred_element_type=F32)
            total = total.reshape(4, 4, 8, 128)
            for z in range(4):
                ob[:, pa, pl.ds(pb * 8 + 2 * z + pc, 8, stride=16), :] = total[:, z]
        for x in range(8):
            out_ref[x] = (field_v[x].astype(F32) + ob[x // 2, x % 2]).astype(BF16)

        r1[:, :, 7] = jnp.zeros((2, 8, 16, 128), BF16)
        for h in range(2):
            for i in range(2):
                r1[h, 4 * i : 4 * i + 4, 0:7] = rs_last(g, a2, a3, 7, 0, first, relays, h, i)
        first = rs_first(r1, b1, b2, 2, 1)

        finish_y(dp_b, dp_r, dp_y)
        for k in range(27):
            for h in range(2):
                di[:, k * 256 + h * 128 : k * 256 + (h + 1) * 128] = tap(dp_b, h, k // 9, k // 3 % 3, k % 3)

        relays = rs_relay(r1, b1, b3s, b3, 2, 1, first)

        total = jnp.zeros((128, 128), F32)
        for k in range(27):
            total = total + lax.dot_general(
                di[:, k * 256 : (k + 1) * 256], w1[26 - k], (((1,), (1,)), ((), ())), preferred_element_type=F32
            )
        total = (total * 0.125).reshape(4, 4, 8, 128)
        for z in range(4):
            for j in range(4):
                fg[:, pl.ds(j // 2 * 8 + 2 * z + j % 2, 8, stride=16), :] = total[:, z]
        for x in range(8):
            grad_ref[x] = (cot_v[x].astype(F32) + fg[x // 2]).astype(BF16)

        for h in range(2):
            for i in range(2):
                r2[4 * i : 4 * i + 4, h] = rs_last(r1, b2, b3, 2, 1, first, relays, h, i)

        ups = []
        for d in range(1, nz):
            ups.append(
                remote(
                    r2.at[lax.rem(gz + d, nz)], zb.at[gz], z_send.at[d - 1], z_recv.at[d - 1], at(0, 0, d)
                )
            )
        sent.extend(ups)
        zb[gz] = r2[gz]
        for copy in ups:
            copy.wait_recv()
        total = zb[0].astype(F32)
        for j in range(1, nz):
            total = total + zb[j].astype(F32)
        scale = jnp.where(core == 0, F32(1.0 / math.sqrt(cells)), F32(1.0 / math.sqrt(cells / 8.0)))
        mine = chip * ny + gy
        ag[core, mine] = total * scale

        gathers = []
        for dx in range(chips):
            for dy in range(ny):
                if (dx, dy) != (0, 0):
                    n = dx * ny + dy - 1
                    gathers.append(
                        remote(
                            ag.at[core, mine], ag.at[core, mine], ag_send.at[n], ag_recv.at[n], at(2 * dx, dy, 0)
                        )
                    )
        sent.extend(gathers)
        for copy in gathers:
            copy.wait_recv()
        last = remote(ag.at[core], ag.at[core], pair_send.at[2], pair_recv.at[2], other)
        sent.extend((pair_im, pair_hb, last))
        last.wait_recv()
        for k in range(27):
            j = k % 7
            for h in range(2):
                src = k // 7 * 4 + j // 2 if h == 0 else j // 2 * 4 + k // 7
                fine_ref[k, :, h * 128 : (h + 1) * 128] = ag[0, src, h, j % 2]
                coarse_ref[k, 16 * h : 16 * h + 16, :] = ag[1, src, h, j % 2]
        for copy in sent:
            copy.wait_send()

    return kernel


def solution(mesh):
    sizes = (mesh.shape["gx"], mesh.shape["gy"], mesh.shape["gz"])
    dma = pltpu.SemaphoreType.DMA

    def local(field, coarse_weight, fine_weight, cotangent):
        v = pltpu.VMEM
        scratch = [
            v((8, 128, 128), BF16), v((8, 128, 128), BF16), v((27, 128, 256), BF16), v((27, 256, 128), BF16),
            v((8, 4, 512, 128), BF16),
            v((10, 192, 128), F32), v((2, 10, 24, 128), F32), v((2, 10, 24, 128), F32), v((4, 64, 128), F32),
            v((1, 6, 6, 24, 128), F32), v((2, 1, 40, 128), F32), v((2, 1, 40, 128), F32),
            v((2, 6, 6, 24, 128), F32), v((2, 2, 40, 128), F32), v((2, 2, 40, 128), F32),
            v((2, 6, 6, 24, 128), F32), v((2, 2, 40, 128), F32), v((2, 2, 40, 128), F32),
            v((2, 256, 3456), BF16), v((2, 256, 256), BF16), v((128, 6912), BF16), v((128, 6912), BF16),
            v((4, 2, 128, 128), F32), v((4, 128, 128), F32),
            v((2, 8, 28, 16, 128), BF16),
            v((2, 2, 4, 7, 16, 128), BF16), v((2, 2, 4, 7, 16, 128), BF16),
            v((2, 2, 4, 7, 16, 128), BF16), v((2, 2, 4, 7, 16, 128), BF16),
            v((2, 8, 8, 16, 128), BF16),
            v((2, 2, 4, 2, 16, 128), BF16), v((2, 2, 4, 2, 16, 128), BF16),
            v((2, 2, 4, 2, 16, 128), BF16), v((2, 2, 4, 2, 16, 128), BF16),
            v((8, 2, 2, 16, 128), BF16), v((8, 2, 2, 16, 128), BF16), v((2, 16, 2, 2, 16, 128), F32),
            dma((4,)), dma((4, 10)), dma((4, 10)), dma((3,)), dma((3,)),
            dma((2, 2, 2, 3)), dma((2, 2, 2, 3)), dma((7,)), dma((7,)), dma((15,)), dma((15,)),
        ]
        anywhere = pl.BlockSpec(memory_space=pl.ANY)
        inside = pl.BlockSpec(memory_space=pltpu.VMEM)
        output, field_grad, fine, coarse = pl.pallas_call(
            make_kernel(sizes),
            out_shape=(
                jax.ShapeDtypeStruct((8, 128, 128), BF16),
                jax.ShapeDtypeStruct((8, 128, 128), BF16),
                jax.ShapeDtypeStruct((27, 16, 256), F32),
                jax.ShapeDtypeStruct((27, 32, 128), F32),
            ),
            in_specs=[anywhere] * 4,
            out_specs=(inside,) * 4,
            scratch_shapes=scratch,
            compiler_params=pltpu.CompilerParams(
                collective_id=0, has_side_effects=True, vmem_limit_bytes=56 * 1024 * 1024
            ),
        )(field.reshape(8, 128, 128), coarse_weight, fine_weight, cotangent.reshape(8, 128, 128))
        return (
            output.reshape(8, 16, 8, 128),
            field_grad.reshape(8, 16, 8, 128),
            fine.transpose(0, 2, 1),
            coarse.transpose(0, 2, 1),
        )

    placed = (P("gx", "gy", "gz", None), P(), P(), P("gx", "gy", "gz", None))
    return jax.shard_map(
        local,
        mesh=mesh,
        in_specs=placed,
        out_specs=(
            P("gx", "gy", "gz", None),
            P("gx", "gy", "gz", None),
            P(None, None, "gz"),
            P(None, None, "gz"),
        ),
        check_vma=False,
    )
```

profile of v0, /device:TPU:1, one launch (start us, length us, event | category | flops | bytes accessed | tf_op | source)
XLA Modules:
  0.0 66.3 jit_solution(11443063608595846700)
XLA Ops:
  0.6 59.7 %shard_map.75 = (bf16[8,128,128]{2,1,0:T(8,128)(2,1)}, bf16[8,128,128]{2,1,0:T(8,128)(2,1)}, f32[27,16,256]{2,1,0:T(8,128)}, f32[27,32,128]{2,1,0:T(8,128)}) custom-call(bf16[8,128,128]{2,1,0:T(8,128)(2,1)} %bitcast.8, bf16[27,128,256]{2,1,0:T(8,128)(2,1)} %w1_hbm.1, bf16[27,256,128]{2,1,0:T(8,128)(2,1)} %w2_hbm.1, bf16[8,128,128]{2,1,0:T(8,128)(2,1)} %bitcast.9), custom_call_target="tpu_custom_call" | custom-call | tf_op jit(solution)/shard_map/pallas_call | solution.py:483
  60.3 0.0 copy-start
  60.3 1.7 %copy.12 = bf16[8,16,8,128]{3,2,1,0:T(8,128)(2,1)} copy(bf16[8,16,8,128]{3,2,1,0:T(8,128)(2,1)} %bitcast.11) | data formatting | bytes 524288
  62.0 1.7 %copy.13 = bf16[8,16,8,128]{3,2,1,0:T(8,128)(2,1)} copy(bf16[8,16,8,128]{3,2,1,0:T(8,128)(2,1)} %bitcast.10) | data formatting | bytes 524288
  63.7 1.8 %copy.14 = f32[27,256,16]{1,2,0:T(8,128)} copy(f32[27,256,16]{1,2,0:T(8,128)} %bitcast.7) | data formatting | bytes 884736
  65.5 0.0 copy-done
  65.5 0.8 %copy.15 = f32[27,128,32]{1,2,0:T(8,128)} copy(f32[27,128,32]{1,2,0:T(8,128)S(1)} %bitcast.6) | data formatting | bytes 884736
Async XLA Ops:
  60.3 5.2 %copy-start = (f32[27,32,128]{2,1,0:T(8,128)S(1)}, f32[27,32,128]{2,1,0:T(8,128)}, u32[]{:S(2)}) copy-start(f32[27,32,128]{2,1,0:T(8,128)} %get-tuple-element.11) | copy-start | bytes 1327108
where the time goes:
time: 66.5 us; the launch traced here: 66.3 us
  Pallas kernels  59.7 us (90%)
  local copies, waits for them, and re-layouts  5.96 us (9%)
    pallas_call x1, Pallas kernels, local(): pl.pallas_call(make_kernel(sizes), out_shape=(jax.ShapeDtypeStruct((8, 12...  59.7 us
    unnamed x6, local copies, waits for them, and re-layouts  5.96 us

commit v1 on v0

v1 whole, which is shorter than its diff:
```python
import math

import jax
import jax.numpy as jnp
from jax import lax
from jax.experimental import pallas as pl
from jax.experimental.pallas import tpu as pltpu
from jax.sharding import PartitionSpec as P

MESH = pl.DeviceIdType.MESH
F32 = jnp.float32
BF16 = jnp.bfloat16

SIDES = (-1, 0, 1)
EIGHT = [(i, j) for i in SIDES for j in SIDES if (i, j) != (0, 0)]
NEAR = sorted(((i, j, k) for i in SIDES for j in SIDES for k in SIDES if (i, j, k) != (0, 0, 0)), key=lambda p: -sum(map(abs, p)))
PAIRS = ((0,), (1, 2), (0, 1), (2,))


def from_side(step, length):
    return pl.ds(1, length) if step == 0 else pl.ds(length if step > 0 else 1, 1)


def to_side(step, length):
    return pl.ds(1, length) if step == 0 else pl.ds(0 if step > 0 else length + 1, 1)


def make_kernel(sizes):
    nx, ny, nz = sizes
    chips = nx // 2
    cells = 1024 * nx * ny * nz

    def kernel(
        field_hbm, w1_hbm, w2_hbm, cot_hbm,
        out_hbm, grad_hbm, ag,
        field_v, cot_v, w1, w2, wc, out_v, grad_v,
        cp, zs, zq, tmp, pool_b, hid_b, hid_s, hid_r, dp_b, dp_s, dp_r,
        im, hb, hi, di, ob, fg,
        g, a1, a2, a3s, a3, r1, gb, r2, zb,
        in_sem, out_sem, halo_send, halo_recv, pair_send, pair_recv, fwd_send, fwd_recv, rs_send, rs_recv, z_send, z_recv, ag_send, ag_recv,
    ):
        gx, gy, gz = lax.axis_index("gx"), lax.axis_index("gy"), lax.axis_index("gz")
        core = lax.rem(gx, 2)
        chip = gx // 2

        def at(dx, dy, dz):
            return (
                lax.rem(gx + (dx + nx), nx),
                lax.rem(gy + (dy + ny), ny),
                lax.rem(gz + (dz + nz), nz),
            )

        def plan(src, dst, send, recv, device):
            return pltpu.make_async_remote_copy(
                src_ref=src, dst_ref=dst, send_sem=send, recv_sem=recv, device_id=device, device_id_type=MESH
            )

        def remote(*where):
            copy = plan(*where)
            copy.start()
            return copy

        other = (gx + 1 - 2 * core, gy, gz)
        sent = []

        def drain():
            for copy in sent:
                copy.wait_send()
            sent.clear()

        def hops(p):
            return min(p[0], chips - p[0]) + min(p[1], ny - p[1])

        loads = [
            pltpu.make_async_copy(src, dst, in_sem.at[i])
            for i, (src, dst) in enumerate(
                ((field_hbm, field_v), (cot_hbm, cot_v), (w2_hbm, w2), (w1_hbm, w1))
            )
        ]
        for load in loads:
            load.start()

        partners = {(i % nx, j % ny, k % nz) for i, j, k in NEAR}
        partners |= {(0, 0, k) for k in range(1, nz)}
        partners |= {(2 * i, j, 0) for i in range(chips) for j in range(ny) if (i, j) != (0, 0)}
        crossing = sorted(((i, j) for i in range(chips) for j in range(ny) if hops((i, j)) > 2))
        barrier = pltpu.get_barrier_semaphore()
        for step in sorted(partners):
            pl.semaphore_signal(barrier, inc=1, device_id=at(*step), device_id_type=MESH)
        for i, j in crossing:
            x, y, z = at(2 * i, j, 0)
            pl.semaphore_signal(barrier, inc=1, device_id=(x + 1 - 2 * core, y, z), device_id_type=MESH)

        loads[0].wait()
        for x in range(4):
            pair = field_v[2 * x].astype(F32) + field_v[2 * x + 1].astype(F32)
            pair = pair.reshape(8, 2, 8, 128)
            tmp[x] = (pair[:, 0] + pair[:, 1]).reshape(64, 128)
        for z in range(4):
            total = tmp[:, pl.ds(2 * z, 8, stride=8), :] + tmp[:, pl.ds(2 * z + 1, 8, stride=8), :]
            pool_b[0, 1:5, 1 + z, 8:16, :] = (total * 0.125).astype(BF16).astype(F32)
        loads[1].wait()
        for x in range(8):
            cp[1 + x, 8:136, :] = cot_v[x].astype(F32)
        zs[0] = cp[1:9, pl.ds(8, 16, stride=8), :]
        zs[1] = cp[1:9, pl.ds(15, 16, stride=8), :]

        pl.semaphore_wait(barrier, len(partners) + len(crossing))

        def start_xz(buf, e):
            copies = []
            for i, (dx, dz) in enumerate(EIGHT):
                copies.append(
                    remote(
                        buf.at[:, from_side(dx, 4), from_side(dz, 4), pl.ds(8, 8), :],
                        buf.at[:, to_side(dx, 4), to_side(dz, 4), pl.ds(8, 8), :],
                        halo_send.at[e, i], halo_recv.at[e, i], at(dx, 0, dz),
                    )
                )
            sent.extend(copies)
            return copies

        def start_y(buf, s, r, e, copies):
            for copy in copies:
                copy.wait_recv()

            @pl.when(gx == 0)
            def _():
                buf[:, 0, :, 8:16, :] = jnp.zeros_like(buf[:, 0, :, 8:16, :])

            @pl.when(gx == nx - 1)
            def _():
                buf[:, 5, :, 8:16, :] = jnp.zeros_like(buf[:, 5, :, 8:16, :])

            @pl.when(gz == 0)
            def _():
                buf[:, :, 0, 8:16, :] = jnp.zeros_like(buf[:, :, 0, 8:16, :])

            @pl.when(gz == nz - 1)
            def _():
                buf[:, :, 5, 8:16, :] = jnp.zeros_like(buf[:, :, 5, 8:16, :])

            flat = buf.reshape(buf.shape[0], 864, 128)
            for h in range(buf.shape[0]):
                s[0, h, 0:36, :] = flat[h, pl.ds(8, 36, stride=24), :]
                s[1, h, 0:36, :] = flat[h, pl.ds(15, 36, stride=24), :]
            below = remote(s.at[0], r.at[1], halo_send.at[e, 8], halo_recv.at[e, 8], at(0, -1, 0))
            above = remote(s.at[1], r.at[0], halo_send.at[e, 9], halo_recv.at[e, 9], at(0, 1, 0))
            sent.extend((below, above))
            return (above, below)

        def finish_y(buf, r, copies):
            for copy in copies:
                copy.wait_recv()

            @pl.when(gy == 0)
            def _():
                r[0] = jnp.zeros_like(r[0])

            @pl.when(gy == ny - 1)
            def _():
                r[1] = jnp.zeros_like(r[1])

            flat = buf.reshape(buf.shape[0], 864, 128)
            for h in range(buf.shape[0]):
                flat[h, pl.ds(7, 36, stride=24), :] = r[0, h, 0:36, :]
                flat[h, pl.ds(16, 36, stride=24), :] = r[1, h, 0:36, :]

        def tap(buf, h, a, b, c):
            return buf[h, a : a + 4, c : c + 4, 7 + b : 15 + b, :].reshape(128, 128).astype(BF16)

        def send_pool(i):
            dx, dy, dz = NEAR[i]
            return remote(
                pool_b.at[:, from_side(dx, 4), from_side(dz, 4), pl.ds(8, 8), :],
                pool_b.at[:, to_side(dx, 4), to_side(dz, 4), pl.ds(8 - 8 * dy, 8), :],
                halo_send.at[0, i], halo_recv.at[0, i], at(dx, dy, dz),
            )

        def send_cot(i):
            dx, dy, dz = NEAR[i]
            if dz == 0:
                sy = pl.ds(8, 128) if dy == 0 else pl.ds(128 if dy > 0 else 8, 8)
                ty = pl.ds(8, 128) if dy == 0 else pl.ds(0 if dy > 0 else 136, 8)
                src, dst = cp.at[from_side(dx, 8), sy, :], cp.at[to_side(dx, 8), ty, :]
            else:
                sx = pl.ds(0, 8) if dx == 0 else pl.ds(7 if dx > 0 else 0, 1)
                sy = pl.ds(0, 16) if dy == 0 else pl.ds(8 if dy > 0 else 0, 8)
                ty = pl.ds(8, 16) if dy == 0 else pl.ds(0 if dy > 0 else 24, 8)
                src = zs.at[1 if dz > 0 else 0, sx, sy, :]
                dst = zq.at[0 if dz > 0 else 1, to_side(dx, 8), ty, :]
            return remote(src, dst, halo_send.at[3, i], halo_recv.at[3, i], at(dx, dy, dz))

        wide = [i for i, (dx, dy, dz) in enumerate(NEAR) if (dx, dy) == (0, 0)]
        cots = [send_cot(i) for i in wide]
        pools = [send_pool(i) for i in range(26)]
        cots += [send_cot(i) for i in range(26) if i not in wide]
        sent.extend(pools + cots)

        loads[2].wait()

        def combine(i, carry):
            rows = pl.ds(pl.multiple_of(i * 16, 16), 16)
            low = pl.ds(pl.multiple_of(i * 16, 16), 16)
            high = pl.ds(pl.multiple_of(256 + i * 16, 16), 16)

            def spread(parts):
                return (parts[0], parts[1] + parts[2], parts[0] + parts[1], parts[2])

            by_ab = [[spread([w2[9 * a + 3 * b + c, rows, :].astype(F32) for c in range(3)]) for b in range(3)] for a in range(3)]
            by_a = [[spread([by_ab[a][b][c] for b in range(3)]) for c in range(4)] for a in range(3)]
            for b in range(4):
                for c in range(4):
                    for a, value in enumerate(spread([by_a[a][c][b] for a in range(3)])):
                        parity = (a // 2) * 4 + (b // 2) * 2 + c // 2
                        wc[parity, (a % 2) * 2 + b % 2, high if c % 2 else low, :] = value.astype(BF16)
            return carry

        lax.fori_loop(0, 16, combine, 0)

        for copy in pools:
            copy.wait_recv()

        @pl.when(gx == 0)
        def _():
            pool_b[:, 0] = jnp.zeros_like(pool_b[:, 0])

        @pl.when(gx == nx - 1)
        def _():
            pool_b[:, 5] = jnp.zeros_like(pool_b[:, 5])

        @pl.when(gz == 0)
        def _():
            pool_b[:, :, 0] = jnp.zeros_like(pool_b[:, :, 0])

        @pl.when(gz == nz - 1)
        def _():
            pool_b[:, :, 5] = jnp.zeros_like(pool_b[:, :, 5])

        @pl.when(gy == 0)
        def _():
            pool_b[:, :, :, 0:8, :] = jnp.zeros_like(pool_b[:, :, :, 0:8, :])

        @pl.when(gy == ny - 1)
        def _():
            pool_b[:, :, :, 16:24, :] = jnp.zeros_like(pool_b[:, :, :, 16:24, :])

        for k in range(27):
            im[0, 0:128, k * 128 : (k + 1) * 128] = tap(pool_b, 0, k // 9, k // 3 % 3, k % 3)
        swap_pool = plan(im.at[0, pl.ds(0, 128)], im.at[0, pl.ds(128, 128)], pair_send.at[0], pair_recv.at[0], other)

        @pl.when(core == 0)
        def _():
            swap_pool.start()

        loads[3].wait()
        pre = jnp.dot(im[0, 0:128, :], w1[...].reshape(3456, 256), preferred_element_type=F32)
        sig = 1.0 / (1.0 + jnp.exp(-pre))
        hidden = (pre * sig).astype(BF16)
        slope = sig * (1.0 + pre * (1.0 - sig))
        hb[1, 0:128, :] = hidden
        swap_hidden = plan(hb.at[1, pl.ds(0, 128)], hb.at[1, pl.ds(128, 128)], pair_send.at[1], pair_recv.at[1], other)

        @pl.when(core == 1)
        def _():
            swap_hidden.start()

        wide = hidden.astype(F32).reshape(4, 4, 8, 256)
        hid_b[0, 1:5, 1:5, 8:16, :] = wide[..., 0:128]
        hid_b[1, 1:5, 1:5, 8:16, :] = wide[..., 128:256]
        hid_xz = start_xz(hid_b, 1)

        for copy in cots:
            copy.wait_recv()

        @pl.when(gx == 0)
        def _():
            cp[0] = jnp.zeros_like(cp[0])
            zq[:, 0] = jnp.zeros_like(zq[:, 0])

        @pl.when(gx == nx - 1)
        def _():
            cp[9] = jnp.zeros_like(cp[9])
            zq[:, 9] = jnp.zeros_like(zq[:, 9])

        @pl.when(gy == 0)
        def _():
            cp[:, 0:8, :] = jnp.zeros_like(cp[:, 0:8, :])
            zq[:, :, 0:8, :] = jnp.zeros_like(zq[:, :, 0:8, :])

        @pl.when(gy == ny - 1)
        def _():
            cp[:, 136:144, :] = jnp.zeros_like(cp[:, 136:144, :])
            zq[:, :, 24:32, :] = jnp.zeros_like(zq[:, :, 24:32, :])

        @pl.when(gz == 0)
        def _():
            zq[0] = jnp.zeros_like(zq[0])

        @pl.when(gz == nz - 1)
        def _():
            zq[1] = jnp.zeros_like(zq[1])

        def swap_windows(x):
            rows, theirs = pl.ds(pl.multiple_of(x * 32, 32), 32), pl.ds(pl.multiple_of(128 + x * 32, 32), 32)
            return plan(im.at[1, rows], im.at[1, theirs], pair_send.at[3 + x], pair_recv.at[3 + x], other)

        def windows(x, carry):
            rows = pl.ds(pl.multiple_of(x * 32, 32), 32)
            for a in range(3):
                planes = pl.ds(2 * x + 2 - a, 2)
                sums = []
                for z in range(10):
                    columns = []
                    for y in range(4):
                        if z == 0:
                            value = zq[0, planes, pl.ds(7 + y, 8, stride=2), :]
                        elif z == 9:
                            value = zq[1, planes, pl.ds(7 + y, 8, stride=2), :]
                        else:
                            value = cp[planes, pl.ds(y * 8 + z - 1, 8, stride=16), :]
                        columns.append(value[0] + value[1])
                    sums.append([columns[2 - b] + columns[3 - b] for b in range(3)])
                for b in range(3):
                    for c in range(3):
                        k = 9 * a + 3 * b + c
                        value = jnp.concatenate(
                            [sums[2 * z + 2 - c][b] + sums[2 * z + 3 - c][b] for z in range(4)], axis=0
                        )
                        im[1, rows, k * 128 : (k + 1) * 128] = value.astype(BF16)

            @pl.when(core == 1)
            def _():
                swap_windows(x).start()

            return carry

        lax.fori_loop(0, 4, windows, 0)

        d_hidden = jnp.zeros((128, 256), F32)
        for k in range(27):
            d_hidden = d_hidden + lax.dot_general(
                im[1, 0:128, k * 128 : (k + 1) * 128], w2[k], (((1,), (1,)), ((), ())), preferred_element_type=F32
            )
        d_pre = (d_hidden * slope).astype(BF16)
        hb[0, 0:128, :] = d_pre
        swap_d_pre = plan(hb.at[0, pl.ds(0, 128)], hb.at[0, pl.ds(128, 128)], pair_send.at[2], pair_recv.at[2], other)

        @pl.when(core == 0)
        def _():
            swap_d_pre.start()

        def ring(axis, step):
            return at(2 * step, 0, 0) if axis == 0 else at(0, step, 0)

        def place(axis, step):
            return lax.rem(chip + (step + 4), 4) if axis == 0 else lax.rem(gy + (step + 4), 4)

        BOTH = [(h, i, d) for h in range(2) for i, d in enumerate((1, -1))]

        def block(h, i, step):
            return g.at[h, pl.ds(4 * i, 4), pl.ds(7 * place(h, step), 7)]

        def ring_start():
            opposite = {
                (h, i): remote(
                    block(h, i, 2), a1.at[h, i], rs_send.at[0, h, i], rs_recv.at[0, h, i], ring(h, d)
                )
                for h, i, d in BOTH
            }
            nearest = {
                (h, i): remote(
                    block(h, 1 - i, d), a2.at[h, i], rs_send.at[1, h, i], rs_recv.at[1, h, i], ring(h, d)
                )
                for h, i, d in BOTH
            }
            sent.extend([*opposite.values(), *nearest.values()])
            return opposite, nearest

        def ring_relay(opposite):
            relays = {}
            for h, i, d in BOTH:
                opposite[h, i].wait_recv()
                a3s[h, i] = (block(h, i, d)[...].astype(F32) + a1[h, i].astype(F32)).astype(BF16)
                relays[h, i] = remote(a3s.at[h, i], a3.at[h, i], rs_send.at[2, h, i], rs_recv.at[2, h, i], ring(h, d))
            sent.extend(relays.values())
            return relays

        def ring_end(nearest, relays):
            for h, i, d in BOTH:
                nearest[h, 1 - i].wait_recv()
                relays[h, i].wait_recv()
                total = block(h, i, 0)[...].astype(F32) + a2[h, 1 - i].astype(F32) + a3[h, i].astype(F32)
                r1[h, 4 * i : 4 * i + 4, 0:7] = total.astype(BF16)

        def scatter():
            copies = [[], []]
            for step in (2, 1, 3):
                for h in range(2):
                    axis = 1 - h
                    copies[h].append(
                        remote(
                            r1.at[h, :, pl.ds(2 * place(axis, step), 2)], gb.at[h, step - 1],
                            rs_send.at[3 + step - 1, h, 0], rs_recv.at[3 + step - 1, h, 0], ring(axis, step),
                        )
                    )
            sent.extend(copies[0] + copies[1])
            return copies

        def add_up(copies, h):
            for copy in copies[h]:
                copy.wait_recv()
            total = r1[h, :, pl.ds(2 * place(1 - h, 0), 2)].astype(F32)
            for step in range(3):
                total = total + gb[h, step].astype(F32)
            r2[:, h] = total.astype(BF16)

        wide = d_pre.astype(F32).reshape(4, 4, 8, 256)
        dp_b[0, 1:5, 1:5, 8:16, :] = wide[..., 0:128]
        dp_b[1, 1:5, 1:5, 8:16, :] = wide[..., 128:256]
        dp_xz = start_xz(dp_b, 2)
        hid_y = start_y(hid_b, hid_s, hid_r, 1, hid_xz)

        g[:, :, 27] = jnp.zeros((2, 8, 16, 128), BF16)

        @pl.when(core == 0)
        def _():
            swap_hidden.wait_recv()
            for x in range(4):
                swap_windows(x).wait_recv()
            right = hb[1]
            for k in range(27):
                value = lax.dot_general(
                    im[1, :, k * 128 : (k + 1) * 128], right, (((0,), (0,)), ((), ())), preferred_element_type=F32
                ).astype(BF16)
                value = value.reshape(8, 16, 256)
                g[0, :, k] = value[..., 0:128]
                g[1, :, k] = value[..., 128:256]

        @pl.when(core == 1)
        def _():
            swap_pool.wait_recv()
            swap_d_pre.wait_recv()
            left = hb[0].astype(F32).T.astype(BF16)
            for k in range(27):
                value = jnp.dot(left, im[0, :, k * 128 : (k + 1) * 128], preferred_element_type=F32).astype(BF16)
                value = value.reshape(8, 2, 16, 128)
                g[0, :, k] = value[:, 0]
                g[1, :, k] = value[:, 1]

        opposite, nearest = ring_start()
        dp_y = start_y(dp_b, dp_s, dp_r, 2, dp_xz)
        relays = ring_relay(opposite)


        finish_y(hid_b, hid_r, hid_y)
        for k in range(27):
            for h in range(2):
                hi[:, k * 256 + h * 128 : k * 256 + (h + 1) * 128] = tap(hid_b, h, k // 9, k // 3 % 3, k % 3)

        for parity in range(8):
            pa, pb, pc = parity // 4, parity // 2 % 2, parity % 2
            total = jnp.zeros((128, 128), F32)
            for side in range(4):
                k = 9 * (pa + side // 2) + 3 * (pb + side % 2) + pc
                total = total + jnp.dot(hi[:, k * 256 : k * 256 + 512], wc[parity, side], preferred_element_type=F32)
            total = total.reshape(4, 4, 8, 128)
            for z in range(4):
                ob[:, pa, pl.ds(pb * 8 + 2 * z + pc, 8, stride=16), :] = total[:, z]
        for x in range(8):
            out_v[x] = (field_v[x].astype(F32) + ob[x // 2, x % 2]).astype(BF16)

        out_copy = pltpu.make_async_copy(out_v, out_hbm, out_sem.at[0])
        out_copy.start()
        drain()

        @pl.when(core == 0)
        def _():
            swap_pool.wait_send()
            swap_d_pre.wait_send()

        @pl.when(core == 1)
        def _():
            swap_hidden.wait_send()
            for x in range(4):
                swap_windows(x).wait_send()

        r1[:, :, 7] = jnp.zeros((2, 8, 16, 128), BF16)
        ring_end(nearest, relays)
        second = scatter()

        for h in range(2):
            add_up(second, h)

        ups = []
        for d in range(1, nz):
            ups.append(
                remote(
                    r2.at[lax.rem(gz + d, nz)], zb.at[gz], z_send.at[d - 1], z_recv.at[d - 1], at(0, 0, d)
                )
            )
        sent.extend(ups)
        zb[gz] = r2[gz]

        finish_y(dp_b, dp_r, dp_y)
        for k in range(27):
            for h in range(2):
                di[:, k * 256 + h * 128 : k * 256 + (h + 1) * 128] = tap(dp_b, h, k // 9, k // 3 % 3, k % 3)

        total = jnp.zeros((128, 128), F32)
        for k in range(27):
            total = total + lax.dot_general(
                di[:, k * 256 : (k + 1) * 256], w1[26 - k], (((1,), (1,)), ((), ())), preferred_element_type=F32
            )
        total = (total * 0.125).reshape(4, 4, 8, 128)
        for z in range(4):
            for j in range(4):
                fg[:, pl.ds(j // 2 * 8 + 2 * z + j % 2, 8, stride=16), :] = total[:, z]
        for x in range(8):
            grad_v[x] = (cot_v[x].astype(F32) + fg[x // 2]).astype(BF16)

        grad_copy = pltpu.make_async_copy(grad_v, grad_hbm, out_sem.at[1])
        grad_copy.start()
        drain()
        for copy in ups:
            copy.wait_recv()
        total = zb[0].astype(F32)
        for j in range(1, nz):
            total = total + zb[j].astype(F32)
        scale = jnp.where(core == 0, F32(1.0 / math.sqrt(cells)), F32(1.0 / math.sqrt(cells / 8.0)))
        mine = chip * ny + gy
        ag[core, mine] = (total * scale).astype(BF16)

        steps = sorted(((i, j) for i in range(chips) for j in range(ny)), key=hops)
        swap = 1 - 2 * core
        drain()

        def spread_to(n, cross):
            dx, dy = steps[n]
            x, y, z = at(2 * dx, dy, 0)
            i = n + 16 * cross
            return remote(
                ag.at[core, mine], ag.at[core, mine], ag_send.at[i], ag_recv.at[i], (x + swap * cross, y, z)
            )

        gathers = {}
        for n in reversed(range(1, 16)):
            gathers[n, 0] = spread_to(n, 0)
            if hops(steps[n]) > 2:
                gathers[n, 1] = spread_to(n, 1)
        sent.extend(gathers.values())
        for n, (dx, dy) in enumerate(steps):
            if hops(steps[n]) <= 2:
                if n > 0:
                    gathers[n, 0].wait_recv()
                came = lax.rem(chip + chips - dx, chips) * ny + lax.rem(gy + ny - dy, ny)
                gathers[n, 2] = remote(ag.at[core, came], ag.at[core, came], fwd_send.at[n], fwd_recv.at[n], other)
                sent.append(gathers[n, 2])
        out_copy.wait()
        grad_copy.wait()
        for (n, way), copy in gathers.items():
            if n == 0 or hops(steps[n]) > 2 or way == 2:
                copy.wait_recv()
        drain()

    return kernel


def finish(out_in, grad_in, ag, out_ref, grad_ref, fine_ref, coarse_ref):
    out_ref[...] = out_in[...]
    grad_ref[...] = grad_in[...]
    for k in range(27):
        j = k % 7
        for h in range(2):
            src = k // 7 * 4 + j // 2 if h == 0 else j // 2 * 4 + k // 7
            fine_ref[k, :, h * 128 : (h + 1) * 128] = ag[0, src, h, j % 2].astype(F32)
            coarse_ref[k, 16 * h : 16 * h + 16, :] = ag[1, src, h, j % 2].astype(F32)


def solution(mesh):
    sizes = (mesh.shape["gx"], mesh.shape["gy"], mesh.shape["gz"])
    dma = pltpu.SemaphoreType.DMA

    def local(field, coarse_weight, fine_weight, cotangent):
        v = pltpu.VMEM
        scratch = [
            v((8, 128, 128), BF16), v((8, 128, 128), BF16), v((27, 128, 256), BF16), v((27, 256, 128), BF16),
            v((8, 4, 512, 128), BF16), v((8, 128, 128), BF16), v((8, 128, 128), BF16),
            v((10, 144, 128), F32), v((2, 8, 16, 128), F32), v((2, 10, 32, 128), F32), v((4, 64, 128), F32),
            v((1, 6, 6, 24, 128), F32),
            v((2, 6, 6, 24, 128), F32), v((2, 2, 40, 128), F32), v((2, 2, 40, 128), F32),
            v((2, 6, 6, 24, 128), F32), v((2, 2, 40, 128), F32), v((2, 2, 40, 128), F32),
            v((2, 256, 3456), BF16), v((2, 256, 256), BF16), v((128, 6912), BF16), v((128, 6912), BF16),
            v((4, 2, 128, 128), F32), v((4, 128, 128), F32),
            v((2, 8, 28, 16, 128), BF16),
            v((2, 2, 4, 7, 16, 128), BF16), v((2, 2, 4, 7, 16, 128), BF16),
            v((2, 2, 4, 7, 16, 128), BF16), v((2, 2, 4, 7, 16, 128), BF16),
            v((2, 8, 8, 16, 128), BF16), v((2, 3, 8, 2, 16, 128), BF16),
            v((8, 2, 2, 16, 128), BF16), v((8, 2, 2, 16, 128), BF16),
            dma((4,)), dma((2,)), dma((4, 26)), dma((4, 26)), dma((7,)), dma((7,)), dma((16,)), dma((16,)),
            dma((6, 2, 2)), dma((6, 2, 2)), dma((7,)), dma((7,)), dma((32,)), dma((32,)),
        ]
        anywhere = pl.BlockSpec(memory_space=pl.ANY)
        inside = pl.BlockSpec(memory_space=pltpu.VMEM)
        cells = jax.ShapeDtypeStruct((8, 128, 128), BF16)
        output, field_grad, terms = pl.pallas_call(
            make_kernel(sizes),
            out_shape=(cells, cells, jax.ShapeDtypeStruct((2, 16, 2, 2, 16, 128), BF16)),
            in_specs=[anywhere] * 4,
            out_specs=(anywhere, anywhere, inside),
            scratch_shapes=scratch,
            compiler_params=pltpu.CompilerParams(
                collective_id=0, has_side_effects=True, vmem_limit_bytes=56 * 1024 * 1024
            ),
        )(field.reshape(8, 128, 128), coarse_weight, fine_weight, cotangent.reshape(8, 128, 128))
        output, field_grad, fine, coarse = pl.pallas_call(
            finish,
            out_shape=(
                cells,
                cells,
                jax.ShapeDtypeStruct((27, 16, 256), F32),
                jax.ShapeDtypeStruct((27, 32, 128), F32),
            ),
            in_specs=[inside] * 3,
            out_specs=(inside,) * 4,
        )(output, field_grad, terms)
        return (
            output.reshape(8, 16, 8, 128),
            field_grad.reshape(8, 16, 8, 128),
            fine.transpose(0, 2, 1),
            coarse.transpose(0, 2, 1),
        )

    placed = (P("gx", "gy", "gz", None), P(), P(), P("gx", "gy", "gz", None))
    return jax.shard_map(
        local,
        mesh=mesh,
        in_specs=placed,
        out_specs=(
            P("gx", "gy", "gz", None),
            P("gx", "gy", "gz", None),
            P(None, None, "gz"),
            P(None, None, "gz"),
        ),
        check_vma=False,
    )
```

time: 66.5 us -> 60.7 us (0.913)
  local copies, waits for them, and re-layouts: 5.96 us -> 0 us
    unnamed x6 -> x0, local copies, waits for them, and re-layouts: 5.96 us -> none
    pallas_call x1 -> x2, Pallas kernels: 59.7 us -> 60 us  [the longest x1 57.7 us: local(): pl.pallas_call(make_kernel(sizes), out_shape=(cells, cells, jax.ShapeDtyp...]
where the time goes in v1:
time: 60.7 us; the launch traced here: 60.6 us
  Pallas kernels  60 us (99%)
  between operations  0.64 us (1%)
    pallas_call x1, Pallas kernels, local(): pl.pallas_call(make_kernel(sizes), out_shape=(cells, cells, jax.ShapeDtyp...  57.7 us
    pallas_call x1, Pallas kernels, local(): pl.pallas_call(finish, out_shape=(cells, cells, jax.ShapeDtypeStruct((27,...  2.3 us

profile of v1, /device:TPU:1, one launch (start us, length us, event | category | flops | bytes accessed | tf_op | source)
XLA Modules:
  0.0 60.6 jit_solution(3903726380049826046)
XLA Ops:
  0.6 57.7 %shard_map.75 = (bf16[8,128,128]{2,1,0:T(8,128)(2,1)}, bf16[8,128,128]{2,1,0:T(8,128)(2,1)}, bf16[2,16,2,2,16,128]{5,4,3,2,1,0:T(8,128)(2,1)}) custom-call(bf16[8,128,128]{2,1,0:T(8,128)(2,1)} %bitcast.6, bf16[27,128,256]{2,1,0:T(8,128)(2,1)} %w1_hbm.1, bf16[27,256,128]{2,1,0:T(8,128)(2,1)} %w2_hbm.1, bf16[8,128,128]{2,1,0:T(8,128)(2,1)} %bitcast.7), custom_call_target="tpu_custom_call" | custom-call | tf_op jit(solution)/shard_map/pallas_call | solution.py:606
  58.3 2.3 %shard_map.76 = (bf16[8,128,128]{2,1,0:T(8,128)(2,1)}, bf16[8,128,128]{2,1,0:T(8,128)(2,1)}, f32[27,16,256]{2,1,0:T(8,128)}, f32[27,32,128]{2,1,0:T(8,128)}) custom-call(bf16[8,128,128]{2,1,0:T(8,128)(2,1)} %get-tuple-element.11.out_in, bf16[8,128,128]{2,1,0:T(8,128)(2,1)} %get-tuple-element.12.grad_in, bf16[2,16,2,2,16,128]{5,4,3,2,1,0:T(8,128)(2,1)} %get-tuple-element.13.ag), custom_call_target="tpu_custom_call" | custom-call | tf_op jit(solution)/shard_map/pallas_call | solution.py:616

commit v2 on v1

--- a/solution.py
+++ b/solution.py
@@ -83,13 +83,9 @@
         partners = {(i % nx, j % ny, k % nz) for i, j, k in NEAR}
         partners |= {(0, 0, k) for k in range(1, nz)}
         partners |= {(2 * i, j, 0) for i in range(chips) for j in range(ny) if (i, j) != (0, 0)}
-        crossing = sorted(((i, j) for i in range(chips) for j in range(ny) if hops((i, j)) > 2))
         barrier = pltpu.get_barrier_semaphore()
         for step in sorted(partners):
             pl.semaphore_signal(barrier, inc=1, device_id=at(*step), device_id_type=MESH)
-        for i, j in crossing:
-            x, y, z = at(2 * i, j, 0)
-            pl.semaphore_signal(barrier, inc=1, device_id=(x + 1 - 2 * core, y, z), device_id_type=MESH)
 
         loads[0].wait()
         for x in range(4):
@@ -105,7 +101,7 @@
         zs[0] = cp[1:9, pl.ds(8, 16, stride=8), :]
         zs[1] = cp[1:9, pl.ds(15, 16, stride=8), :]
 
-        pl.semaphore_wait(barrier, len(partners) + len(crossing))
+        pl.semaphore_wait(barrier, len(partners))
 
         def start_xz(buf, e):
             copies = []
@@ -191,10 +187,14 @@
                 dst = zq.at[0 if dz > 0 else 1, to_side(dx, 8), ty, :]
             return remote(src, dst, halo_send.at[3, i], halo_recv.at[3, i], at(dx, dy, dz))
 
-        wide = [i for i, (dx, dy, dz) in enumerate(NEAR) if (dx, dy) == (0, 0)]
-        cots = [send_cot(i) for i in wide]
-        pools = [send_pool(i) for i in range(26)]
-        cots += [send_cot(i) for i in range(26) if i not in wide]
+        pools, cots = [], []
+        faces = [i for i in range(26) if sum(map(abs, NEAR[i])) == 1]
+        for i in faces:
+            cots.append(send_cot(i))
+        for i in range(26):
+            pools.append(send_pool(i))
+            if i not in faces:
+                cots.append(send_cot(i))
         sent.extend(pools + cots)
 
         loads[2].wait()
@@ -268,7 +268,6 @@
         wide = hidden.astype(F32).reshape(4, 4, 8, 256)
         hid_b[0, 1:5, 1:5, 8:16, :] = wide[..., 0:128]
         hid_b[1, 1:5, 1:5, 8:16, :] = wide[..., 128:256]
-        hid_xz = start_xz(hid_b, 1)
 
         for copy in cots:
             copy.wait_recv()
@@ -418,8 +417,6 @@
         wide = d_pre.astype(F32).reshape(4, 4, 8, 256)
         dp_b[0, 1:5, 1:5, 8:16, :] = wide[..., 0:128]
         dp_b[1, 1:5, 1:5, 8:16, :] = wide[..., 128:256]
-        dp_xz = start_xz(dp_b, 2)
-        hid_y = start_y(hid_b, hid_s, hid_r, 1, hid_xz)
 
         g[:, :, 27] = jnp.zeros((2, 8, 16, 128), BF16)
 
@@ -449,8 +446,15 @@
                 g[1, :, k] = value[:, 1]
 
         opposite, nearest = ring_start()
+        hid_xz = start_xz(hid_b, 1)
+        dp_xz = start_xz(dp_b, 2)
+        relays = ring_relay(opposite)
+        hid_y = start_y(hid_b, hid_s, hid_r, 1, hid_xz)
         dp_y = start_y(dp_b, dp_s, dp_r, 2, dp_xz)
-        relays = ring_relay(opposite)
+
+        r1[:, :, 7] = jnp.zeros((2, 8, 16, 128), BF16)
+        ring_end(nearest, relays)
+        second = scatter()
 
 
         finish_y(hid_b, hid_r, hid_y)
@@ -458,7 +462,7 @@
             for h in range(2):
                 hi[:, k * 256 + h * 128 : k * 256 + (h + 1) * 128] = tap(hid_b, h, k // 9, k // 3 % 3, k % 3)
 
-        for parity in range(8):
+        def conv(parity):
             pa, pb, pc = parity // 4, parity // 2 % 2, parity % 2
             total = jnp.zeros((128, 128), F32)
             for side in range(4):
@@ -467,33 +471,15 @@
             total = total.reshape(4, 4, 8, 128)
             for z in range(4):
                 ob[:, pa, pl.ds(pb * 8 + 2 * z + pc, 8, stride=16), :] = total[:, z]
-        for x in range(8):
-            out_v[x] = (field_v[x].astype(F32) + ob[x // 2, x % 2]).astype(BF16)
-
-        out_copy = pltpu.make_async_copy(out_v, out_hbm, out_sem.at[0])
-        out_copy.start()
-        drain()
-
-        @pl.when(core == 0)
-        def _():
-            swap_pool.wait_send()
-            swap_d_pre.wait_send()
-
-        @pl.when(core == 1)
-        def _():
-            swap_hidden.wait_send()
-            for x in range(4):
-                swap_windows(x).wait_send()
-
-        r1[:, :, 7] = jnp.zeros((2, 8, 16, 128), BF16)
-        ring_end(nearest, relays)
-        second = scatter()
+
+        for parity in range(4):
+            conv(parity)
 
         for h in range(2):
             add_up(second, h)
 
         ups = []
-        for d in range(1, nz):
+        for d in sorted(range(1, nz), key=lambda d: -min(d, nz - d)):
             ups.append(
                 remote(
                     r2.at[lax.rem(gz + d, nz)], zb.at[gz], z_send.at[d - 1], z_recv.at[d - 1], at(0, 0, d)
@@ -501,6 +487,44 @@
             )
         sent.extend(ups)
         zb[gz] = r2[gz]
+
+        for parity in range(4, 8):
+            conv(parity)
+        for x in range(8):
+            out_v[x] = (field_v[x].astype(F32) + ob[x // 2, x % 2]).astype(BF16)
+
+        out_copy = pltpu.make_async_copy(out_v, out_hbm, out_sem.at[0])
+        out_copy.start()
+        drain()
+
+        @pl.when(core == 0)
+        def _():
+            swap_pool.wait_send()
+            swap_d_pre.wait_send()
+
+        @pl.when(core == 1)
+        def _():
+            swap_hidden.wait_send()
+            for x in range(4):
+                swap_windows(x).wait_send()
+
+
+        for copy in reversed(ups):
+            copy.wait_recv()
+        total = zb[0].astype(F32)
+        for j in range(1, nz):
+            total = total + zb[j].astype(F32)
+        scale = jnp.where(core == 0, F32(1.0 / math.sqrt(cells)), F32(1.0 / math.sqrt(cells / 8.0)))
+        mine = chip * ny + gy
+        ag[core, mine] = (total * scale).astype(BF16)
+
+        steps = sorted(((i, j) for i in range(chips) for j in range(ny)), key=hops)
+
+        gathers = {}
+        for n in reversed(range(1, 16)):
+            dx, dy = steps[n]
+            gathers[n] = remote(ag.at[core, mine], ag.at[core, mine], ag_send.at[n], ag_recv.at[n], at(2 * dx, dy, 0))
+        sent.extend(gathers.values())
 
         finish_y(dp_b, dp_r, dp_y)
         for k in range(27):
@@ -522,45 +546,18 @@
         grad_copy = pltpu.make_async_copy(grad_v, grad_hbm, out_sem.at[1])
         grad_copy.start()
         drain()
-        for copy in ups:
-            copy.wait_recv()
-        total = zb[0].astype(F32)
-        for j in range(1, nz):
-            total = total + zb[j].astype(F32)
-        scale = jnp.where(core == 0, F32(1.0 / math.sqrt(cells)), F32(1.0 / math.sqrt(cells / 8.0)))
-        mine = chip * ny + gy
-        ag[core, mine] = (total * scale).astype(BF16)
-
-        steps = sorted(((i, j) for i in range(chips) for j in range(ny)), key=hops)
-        swap = 1 - 2 * core
-        drain()
-
-        def spread_to(n, cross):
-            dx, dy = steps[n]
-            x, y, z = at(2 * dx, dy, 0)
-            i = n + 16 * cross
-            return remote(
-                ag.at[core, mine], ag.at[core, mine], ag_send.at[i], ag_recv.at[i], (x + swap * cross, y, z)
-            )
-
-        gathers = {}
-        for n in reversed(range(1, 16)):
-            gathers[n, 0] = spread_to(n, 0)
-            if hops(steps[n]) > 2:
-                gathers[n, 1] = spread_to(n, 1)
-        sent.extend(gathers.values())
+
+        forwards = []
         for n, (dx, dy) in enumerate(steps):
-            if hops(steps[n]) <= 2:
-                if n > 0:
-                    gathers[n, 0].wait_recv()
-                came = lax.rem(chip + chips - dx, chips) * ny + lax.rem(gy + ny - dy, ny)
-                gathers[n, 2] = remote(ag.at[core, came], ag.at[core, came], fwd_send.at[n], fwd_recv.at[n], other)
-                sent.append(gathers[n, 2])
+            if n > 0:
+                gathers[n].wait_recv()
+            came = lax.rem(chip + chips - dx, chips) * ny + lax.rem(gy + ny - dy, ny)
+            forwards.append(remote(ag.at[core, came], ag.at[core, came], fwd_send.at[n], fwd_recv.at[n], other))
+        sent.extend(forwards)
         out_copy.wait()
         grad_copy.wait()
-        for (n, way), copy in gathers.items():
-            if n == 0 or hops(steps[n]) > 2 or way == 2:
-                copy.wait_recv()
+        for copy in forwards:
+            copy.wait_recv()
         drain()
 
     return kernel
@@ -598,7 +595,7 @@
             v((2, 8, 8, 16, 128), BF16), v((2, 3, 8, 2, 16, 128), BF16),
             v((8, 2, 2, 16, 128), BF16), v((8, 2, 2, 16, 128), BF16),
             dma((4,)), dma((2,)), dma((4, 26)), dma((4, 26)), dma((7,)), dma((7,)), dma((16,)), dma((16,)),
-            dma((6, 2, 2)), dma((6, 2, 2)), dma((7,)), dma((7,)), dma((32,)), dma((32,)),
+            dma((6, 2, 2)), dma((6, 2, 2)), dma((7,)), dma((7,)), dma((16,)), dma((16,)),
         ]
         anywhere = pl.BlockSpec(memory_space=pl.ANY)
         inside = pl.BlockSpec(memory_space=pltpu.VMEM)

time: 60.7 us -> 58.3 us (0.960)
  Pallas kernels: 60 us -> 57.6 us
    pallas_call x1, Pallas kernels: 57.7 us -> 55.3 us  [local(): pl.pallas_call(make_kernel(sizes), out_shape=(cells, cells, jax.ShapeDtyp...]
where the time goes in v2:
time: 58.3 us; the launch traced here: 58.2 us
  Pallas kernels  57.6 us (99%)
  between operations  0.64 us (1%)
    pallas_call x1, Pallas kernels, local(): pl.pallas_call(make_kernel(sizes), out_shape=(cells, cells, jax.ShapeDtyp...  55.3 us
    pallas_call x1, Pallas kernels, local(): pl.pallas_call(finish, out_shape=(cells, cells, jax.ShapeDtypeStruct((27,...  2.3 us

profile of v2, /device:TPU:1, one launch (start us, length us, event | category | flops | bytes accessed | tf_op | source)
XLA Modules:
  0.0 58.2 jit_solution(14451392569697587)
XLA Ops:
  0.6 55.3 %shard_map.75 = (bf16[8,128,128]{2,1,0:T(8,128)(2,1)}, bf16[8,128,128]{2,1,0:T(8,128)(2,1)}, bf16[2,16,2,2,16,128]{5,4,3,2,1,0:T(8,128)(2,1)}) custom-call(bf16[8,128,128]{2,1,0:T(8,128)(2,1)} %bitcast.6, bf16[27,128,256]{2,1,0:T(8,128)(2,1)} %w1_hbm.1, bf16[27,256,128]{2,1,0:T(8,128)(2,1)} %w2_hbm.1, bf16[8,128,128]{2,1,0:T(8,128)(2,1)} %bitcast.7), custom_call_target="tpu_custom_call" | custom-call | tf_op jit(solution)/shard_map/pallas_call | solution.py:603
  55.9 2.3 %shard_map.76 = (bf16[8,128,128]{2,1,0:T(8,128)(2,1)}, bf16[8,128,128]{2,1,0:T(8,128)(2,1)}, f32[27,16,256]{2,1,0:T(8,128)}, f32[27,32,128]{2,1,0:T(8,128)}) custom-call(bf16[8,128,128]{2,1,0:T(8,128)(2,1)} %get-tuple-element.11.out_in, bf16[8,128,128]{2,1,0:T(8,128)(2,1)} %get-tuple-element.12.grad_in, bf16[2,16,2,2,16,128]{5,4,3,2,1,0:T(8,128)(2,1)} %get-tuple-element.13.ag), custom_call_target="tpu_custom_call" | custom-call | tf_op jit(solution)/shard_map/pallas_call | solution.py:613
